TPU v7x, 256 devices: a whole 4x4x8 slice. The times are simulated.
256 devices in a mesh: blk: 16 (over x_lo, z), dp: 16 (over x_hi, y, core).
Axes of the slice: x: 4 (x_hi: 2, x_lo: 2; x = x_hi * 2 + x_lo), y: 4, z: 8, core: 2. Of those that a mesh axis runs over, the one named last changes fastest.
Arguments:
- user_emb: bfloat16 [65536, 256], P(('blk', 'dp')), may hold values from -6 to 6
- pos_feat: bfloat16 [65536, 256], P(('blk', 'dp')), may hold values from -6 to 6
- pos_id: int32 [65536], P(('blk', 'dp')), may hold values from 0 to 4095
- neg_feat: bfloat16 [131072, 256], P(('blk', 'dp')), may hold values from -6 to 6
- neg_id: int32 [131072], P(('blk', 'dp')), may hold values from 0 to 4095
- neg_bucket: int32 [131072], P(('blk', 'dp')), may hold values from 0 to 1023
- logq_table: float32 [1024], replicated, may hold values from -4 to 0
- w_in: bfloat16 [256, 2048], replicated, may hold values from -0.375 to 0.375
- w_out: bfloat16 [2048, 256], replicated, may hold values from -0.125 to 0.125
Outputs:
- user_grad: float32 [65536, 256], P(('blk', 'dp'))
- w_in_grad: float32 [256, 2048], replicated
- w_out_grad: float32 [2048, 256], replicated
All inputs are finite; a program needn't handle non-finite values.
Results may differ from a plain program's by a relative error of at most 0.008.
Values may be sent and summed in bfloat16 or wider, within the bound.
No kernel may reach another device: no remote copies, remote signals or barrier semaphores. Data moves between devices by JAX's collectives and lax.ppermute only.
A program may use at most 128 MiB of HBM per device.

v0:
```python
import math
import jax
import jax.numpy as jnp
from jax import lax
from jax.sharding import PartitionSpec as P

score_gain = 2.0


def tower(feat, w_in, w_out):
    hidden = jnp.maximum(jnp.dot(feat, w_in, preferred_element_type=jnp.float32), 0.0).astype(
        jnp.bfloat16
    )
    emb = jnp.dot(hidden, w_out, preferred_element_type=jnp.float32).astype(jnp.bfloat16)
    return (hidden, emb)


def tower_grads(feat, hidden, emb_grad, w_out):
    back = jnp.dot(emb_grad, w_out.T, preferred_element_type=jnp.float32)
    back = jnp.where(hidden > 0, back, 0.0).astype(jnp.bfloat16)
    return (
        jnp.dot(feat.T, back, preferred_element_type=jnp.float32),
        jnp.dot(hidden.T, emb_grad, preferred_element_type=jnp.float32),
    )


def on_device(user_emb, pos_feat, pos_id, neg_feat, neg_id, neg_bucket, logq_table, w_in, w_out):
    scale = score_gain / math.sqrt(user_emb.shape[1])
    neg_hidden, neg_emb = tower(neg_feat, w_in, w_out)
    pos_hidden, pos_emb = tower(pos_feat, w_in, w_out)
    pos_score = scale * jnp.einsum(
        "ue,ue->u", user_emb, pos_emb, preferred_element_type=jnp.float32
    )
    pos_exp = jnp.exp(pos_score)
    all_emb, all_ids, all_buckets = (
        lax.all_gather(neg_emb, "blk", axis=0, tiled=True),
        lax.all_gather(neg_id, "blk", axis=0, tiled=True),
        lax.all_gather(neg_bucket, "blk", axis=0, tiled=True),
    )
    all_bias = jnp.take(logq_table, all_buckets)
    scores = (
        scale * jnp.dot(user_emb, all_emb.T, preferred_element_type=jnp.float32) - all_bias[None, :]
    )
    kept = jnp.where(all_ids[None, :] != pos_id[:, None], jnp.exp(scores), jnp.float32(0.0))
    total = pos_exp + jnp.sum(kept, axis=1)
    prob = (kept / total[:, None]).astype(jnp.bfloat16)
    pos_prob = pos_exp / total
    user_grad = scale * jnp.dot(prob, all_emb, preferred_element_type=jnp.float32) + scale * (
        pos_prob - 1.0
    )[:, None] * pos_emb.astype(jnp.float32)
    neg_grad = lax.psum_scatter(
        scale * jnp.dot(prob.T, user_emb, preferred_element_type=jnp.float32),
        "blk",
        scatter_dimension=0,
        tiled=True,
    ).astype(jnp.bfloat16)
    pos_grad = (scale * (pos_prob - 1.0)[:, None] * user_emb.astype(jnp.float32)).astype(
        jnp.bfloat16
    )
    neg_in, neg_out = tower_grads(neg_feat, neg_hidden, neg_grad, w_out)
    pos_in, pos_out = tower_grads(pos_feat, pos_hidden, pos_grad, w_out)
    w_in_grad, w_out_grad = lax.psum((neg_in + pos_in, neg_out + pos_out), ("blk", "dp"))
    return (user_grad, w_in_grad, w_out_grad)


def solution(mesh):
    return jax.shard_map(
        on_device,
        mesh=mesh,
        in_specs=(
            P(("blk", "dp"), None),
            P(("blk", "dp"), None),
            P(("blk", "dp")),
            P(("blk", "dp"), None),
            P(("blk", "dp")),
            P(("blk", "dp")),
            P(),
            P(),
            P(),
        ),
        out_specs=(P(("blk", "dp"), None), P(), P()),
        check_vma=False,
    )
```

profile of v0, /device:TPU:2, one launch (start us, length us, event | category | flops | bytes accessed | tf_op | source)
XLA Modules:
  0.0 515.9 jit_solution(11676487283757321345)
XLA Ops:
  7.2 0.0 copy-start
  7.2 0.0 copy-start.11
  7.2 0.0 copy-start.1
  7.2 0.0 all-gather.4.cloned.1.call-start
  7.2 1.1 copy-done
  8.4 1.7 maximum_convert_fusion
  10.1 0.0 copy-start.3
  10.1 1.3 copy-done.3
  11.4 2.6 convolution_convert_fusion
  14.0 0.0 all-gather.4.cloned.1.call-update
  14.1 0.0 reduce-scatter.2.cloned.1.call-start
  14.1 0.0 copy-done.11
  14.1 35.5 %all-gather.1 = s32[16,1,512]{2,1,0:T(1,128)S(1)} all-gather(s32[1,1,512]{2,1,0:T(1,128)S(1)} %bitcast.33), channel_id=1, replica_groups=mesh['blk'=16,'dp'=16] {'blk'}, dimensions={0}, use_global_device_ids=true | all-gather | bytes 34816 | tf_op jit(solution)/shard_map/all_gather | solution.py:38
  49.6 0.0 copy-done.1
  49.6 0.0 copy-start.12
  49.7 0.0 copy-start.8
  49.7 0.0 copy-start.5
  49.7 0.0 copy-start.6
  49.7 32.9 %gather_fusion = f32[8192]{0:T(1024)S(1)} fusion(f32[1024]{0:T(1024)S(1)} %copy-done.1, s32[8192]{0:T(1024)S(1)} %fusion.22), kind=kCustom, calls=%fused_computation | custom fusion | bytes 98304 | tf_op jit(solution)/shard_map/jit(_take)/gather | solution.py:40
  82.6 0.0 copy-start.13
  82.6 0.0 copy-done.12
  82.6 29.7 %all-gather = s32[16,1,512]{2,1,0:T(1,128)S(1)} all-gather(s32[1,1,512]{2,1,0:T(1,128)S(1)} %bitcast.34), channel_id=1, replica_groups=mesh['blk'=16,'dp'=16] {'blk'}, dimensions={0}, use_global_device_ids=true | all-gather | bytes 34816 | tf_op jit(solution)/shard_map/all_gather | solution.py:37
  112.3 0.0 copy-done.8
  112.3 0.4 fusion.5
  112.8 0.0 copy-start.4
  112.8 1.0 copy-done.4
  113.7 0.0 copy-done.5
  113.8 0.0 copy-done.6
  113.8 1.2 fusion.13
  114.9 0.0 all-gather.4.cloned.1.call-done
  114.9 0.0 copy-done.13
  114.9 6.7 %fusion.28 = (f32[256]{0:T(256)S(1)}, f32[256,8192]{0,1:T(8,128)S(1)}) fusion(f32[8192]{0:T(1024)S(1)} %and_select_fusion, bf16[8192,256]{1,0:T(8,128)(2,1)} %all-gather.4.cloned.1.call-done, bf16[256,256]{1,0:T(8,128)(2,1)S(1)} %copy-done.6, s32[256]{0:T(256)S(1)} %copy-done.13, s32[8192]{0:T(1024)S(1)} %bitcast.32), kind=kOutput, calls=%fused_computation.43 | convolution fusion | flops 1084227328 | bytes 12781568 | tf_op jit(solution)/shard_map/dot_general | solution.py:42
  121.6 0.8 divide_convert_fusion
  122.4 0.0 copy-start.2
  122.4 1.9 copy-done.2
  124.4 4.5 convolution_multiply_fusion
  128.8 0.0 reduce-scatter.2.cloned.1.call-update
  128.9 0.0 all-reduce.3.cloned.1.call-start
  128.9 1.8 fusion.18
  130.7 3.7 fusion.7
  134.4 0.0 copy-start.10
  134.4 93.3 %reduce-scatter.2.cloned.1.call-done = f32[512,256]{1,0:T(8,128)} async-done(((f32[8192,256]{1,0:T(8,128)}), f32[512,256]{1,0:T(8,128)}) %reduce-scatter.2.cloned.1.call-update) | async-done | bytes 524304 | tf_op jit(solution)/shard_map/reduce_scatter | solution.py:51
  227.7 3.7 convolution_add_fusion
  231.5 0.0 copy-done.10
  231.5 5.3 %fusion.4 = f32[256,2048]{0,1:T(8,128)} fusion(f32[2048,256]{1,0:T(8,128)} %fusion.7, bf16[512,256]{1,0:T(8,128)(2,1)S(1)} %copy-done.10, bf16[512,2048]{1,0:T(8,128)(2,1)} %copy-done.3, bf16[2048,256]{1,0:T(8,128)(2,1)} %param.17, f32[512,256]{1,0:T(8,128)} %reduce-scatter.2.cloned.1.call-done), kind=kOutput, calls=%fused_computation.13 | convolution fusion | flops 1077542912 | bytes 8126464 | tf_op jit(solution)/shard_map/dot_general | solution.py:22
  236.8 0.0 copy-start.9
  236.8 0.0 all-reduce.3.cloned.1.call-update
  236.8 0.9 copy-done.9
  237.7 5.5 %fusion.8 = f32[256,256]{1,0:T(8,128)} fusion(bf16[256,8192]{0,1:T(8,128)(2,1)} %copy-done.2, bf16[8192,256]{1,0:T(8,128)(2,1)} %all-gather.4.cloned.1.call-done, f32[256,256]{1,0:T(8,128)S(1)} %copy-done.9, f32[256]{0:T(256)S(1)} %get-tuple-element.14), kind=kOutput, calls=%fused_computation.20 | convolution fusion | flops 1073938432 | bytes 8913920 | tf_op jit(solution)/shard_map/dot_general | solution.py:48
  243.2 261.8 %all-reduce.3.cloned.1.call-done = (f32[256,2048]{0,1:T(8,128)}, f32[2048,256]{1,0:T(8,128)}) async-done(((f32[256,2048]{0,1:T(8,128)}, f32[2048,256]{1,0:T(8,128)}), (f32[256,2048]{0,1:T(8,128)}, f32[2048,256]{1,0:T(8,128)})) %all-reduce.3.cloned.1.call-update) | async-done | bytes 4194320 | tf_op jit(solution)/shard_map/psum | solution.py:62
  505.0 0.0 copy-start.7
  505.0 3.0 copy.14
  508.0 0.0 copy-done.7
  508.0 1.3 copy.22
  (3 shorter events, 0.0 us)
Async XLA Ops:
  7.2 1.2 copy-start
  7.2 6.9 %copy-start.11 = (s32[512]{0:T(512)S(1)}, s32[512]{0:T(512)}, u32[]{:S(2)}) copy-start(s32[512]{0:T(512)} %param.14) | copy-start | bytes 6148
  7.2 42.4 %copy-start.1 = (f32[1024]{0:T(1024)S(1)}, f32[1024]{0:T(1024)}, u32[]{:S(2)}) copy-start(f32[1024]{0:T(1024)} %param.15) | copy-start | bytes 12292
  7.2 107.7 %all-gather.4.cloned.1.call-start = ((), (), s32[]{:S(2)}) async-start(), calls=%async_computation.1 | async-start | bytes 4456448 | tf_op jit(solution)/shard_map/all_gather | solution.py:36
  10.1 1.3 copy-start.3
  14.1 213.6 %reduce-scatter.2.cloned.1.call-start = ((), (), s32[]{:S(2)}) async-start(), calls=%async_computation.2 | async-start | bytes 8912896 | tf_op jit(solution)/shard_map/reduce_scatter | solution.py:51
  49.6 32.9 %copy-start.12 = (s32[512]{0:T(512)S(1)}, s32[512]{0:T(512)}, u32[]{:S(2)}) copy-start(s32[512]{0:T(512)} %param.13) | copy-start | bytes 6148
  49.7 62.7 %copy-start.8 = (bf16[256,256]{1,0:T(8,128)(2,1)S(1)}, bf16[256,256]{1,0:T(8,128)(2,1)}, u32[]{:S(2)}) copy-start(bf16[256,256]{1,0:T(8,128)(2,1)} %param.10) | copy-start | bytes 393220
  49.7 64.1 %copy-start.5 = (bf16[2048,256]{1,0:T(8,128)(2,1)S(1)}, bf16[2048,256]{1,0:T(8,128)(2,1)}, u32[]{:S(2)}) copy-start(bf16[2048,256]{1,0:T(8,128)(2,1)} %param.17) | copy-start | bytes 3145732
  49.7 64.1 %copy-start.6 = (bf16[256,256]{1,0:T(8,128)(2,1)S(1)}, bf16[256,256]{1,0:T(8,128)(2,1)}, u32[]{:S(2)}) copy-start(bf16[256,256]{1,0:T(8,128)(2,1)} %param.9) | copy-start | bytes 393220
  82.6 32.3 %copy-start.13 = (s32[256]{0:T(256)S(1)}, s32[256]{0:T(256)}, u32[]{:S(2)}) copy-start(s32[256]{0:T(256)} %param.11) | copy-start | bytes 3076
  112.8 1.0 copy-start.4
  122.4 1.9 copy-start.2
  128.9 376.1 %all-reduce.3.cloned.1.call-start = ((), (), s32[]{:S(2)}) async-start(), calls=%async_computation.3 | async-start | bytes 8388608 | tf_op jit(solution)/shard_map/psum | solution.py:62
  134.4 97.1 %copy-start.10 = (bf16[512,256]{1,0:T(8,128)(2,1)S(1)}, bf16[512,256]{1,0:T(8,128)(2,1)}, u32[]{:S(2)}) copy-start(bf16[512,256]{1,0:T(8,128)(2,1)} %param.12) | copy-start | bytes 786436
  236.8 0.9 copy-start.9
  505.0 3.0 copy-start.7
Sparse Core Ops, SparseCore 0:
  14.2 78.2 all-gather.3
  129.0 98.6 reduce-scatter.1
  236.9 268.0 all-reduce.2
where the time goes:
time: 516 us
  waiting for transfers between devices  355 us (69%)
  blocking collectives  65.2 us (13%)
  local copies, waits for them, and re-layouts  43.6 us (8%)
  matrix products  37.1 us (7%)
  between operations  13.9 us (3%)
    psum x1, waiting for transfers between devices, on_device(): lax.psum((neg_in + pos_in, neg_out + pos_out), ('blk', 'dp'))  262 us
    reduce_scatter x1, waiting for transfers between devices, on_device(): lax.psum_scatter(scale * jnp.dot(prob.T, user_emb, preferred_element_type...  93.3 us
    all_gather x1, blocking collectives, on_device(): lax.all_gather(neg_bucket, 'blk', axis=0, tiled=True)  35.5 us
    gather x1, local copies, waits for them, and re-layouts, on_device(): all_bias = jnp.take(logq_table, all_buckets)  32.9 us
    all_gather x1, blocking collectives, on_device(): lax.all_gather(neg_id, 'blk', axis=0, tiled=True)  29.7 us
    unnamed x30, local copies, waits for them, and re-layouts  10.7 us
  transfers between devices with their start and end apart: 3, of which 2 were waited for; matrix products, arithmetic and copies ran while one was open for 9% of the time, Pallas kernels for 0%

commit v1 on v0

--- a/solution.py
+++ b/solution.py
@@ -34,7 +34,9 @@
     pos_exp = jnp.exp(pos_score)
     all_emb, all_ids, all_buckets = (
         lax.all_gather(neg_emb, "blk", axis=0, tiled=True),
-        lax.all_gather(neg_id, "blk", axis=0, tiled=True),
+        jnp.concatenate(
+            lax.all_to_all(jnp.stack([neg_id] * lax.axis_size("blk")), "blk", 0, 0), axis=0
+        ),
         lax.all_gather(neg_bucket, "blk", axis=0, tiled=True),
     )
     all_bias = jnp.take(logq_table, all_buckets)

time: 516 us -> 495 us (0.959)
  blocking collectives: 65.2 us -> 32.4 us
  starting transfers between devices: 0.12 us -> 10.1 us
    all_gather x1 -> x0, blocking collectives: 29.7 us -> none  [on_device(): lax.all_gather(neg_id, 'blk', axis=0, tiled=True)]
    all_to_all x0 -> x1, starting transfers between devices: none -> 9.94 us  [on_device(): lax.all_to_all(jnp.stack([neg_id] * lax.axis_size('blk')), 'blk', 0, 0)]
  transfers between devices with their start and end apart: 3 -> 4, of which waited for: 2 -> 2; matrix products, arithmetic and copies ran while one was open for 9% -> 9% of each run, Pallas kernels for 0% -> 0%
where the time goes in v1:
time: 495 us; the launch traced here: 494 us
  waiting for transfers between devices  356 us (72%)
  local copies, waits for them, and re-layouts  44.2 us (9%)
  matrix products  37.1 us (7%)
  blocking collectives  32.4 us (7%)
  between operations  14 us (3%)
  starting transfers between devices  10.1 us (2%)
    psum x1, waiting for transfers between devices, on_device(): lax.psum((neg_in + pos_in, neg_out + pos_out), ('blk', 'dp'))  262 us
    reduce_scatter x1, waiting for transfers between devices, on_device(): lax.psum_scatter(scale * jnp.dot(prob.T, user_emb, preferred_element_type...  93.7 us
    gather x1, local copies, waits for them, and re-layouts, on_device(): all_bias = jnp.take(logq_table, all_buckets)  32.9 us
    all_gather x1, blocking collectives, on_device(): lax.all_gather(neg_bucket, 'blk', axis=0, tiled=True)  32.4 us
    unnamed x30, local copies, waits for them, and re-layouts  10.7 us
    all_to_all x1, starting transfers between devices, on_device(): lax.all_to_all(jnp.stack([neg_id] * lax.axis_size('blk')), 'blk', 0, 0)  9.94 us
  transfers between devices with their start and end apart: 4, of which 2 were waited for; matrix products, arithmetic and copies ran while one was open for 9% of the time, Pallas kernels for 0%

profile of v1, /device:TPU:2, one launch (start us, length us, event | category | flops | bytes accessed | tf_op | source)
XLA Modules:
  0.0 494.0 jit_solution(12519154885641123702)
XLA Ops:
  7.2 0.0 copy-start
  7.2 0.0 copy-start.11
  7.2 0.0 copy-start.12
  7.2 0.0 copy-start.1
  7.2 0.0 all-gather.3.cloned.1.call-start
  7.3 1.1 copy-done
  8.4 1.7 maximum_convert_fusion
  10.1 0.0 copy-start.3
  10.1 1.3 copy-done.3
  11.4 2.6 convolution_convert_fusion
  14.0 0.0 all-gather.3.cloned.1.call-update
  14.1 0.0 copy-done.11
  14.1 0.6 stack.2
  14.7 9.9 %all-to-all-start = ((s32[16,1,512]{2,1,0:T(1,128)}), s32[16,1,512]{2,1,0:T(1,128)S(1)}, u32[]{:S(2)}, u32[]{:S(2)}) async-start(s32[16,1,512]{2,1,0:T(1,128)} %stack.2), calls=%async_computation | async-start | bytes 65536 | tf_op jit(solution)/shard_map/all_to_all | solution.py:38
  24.6 0.0 reduce-scatter.2.cloned.1.call-start
  24.7 0.0 copy-done.12
  24.7 32.4 %all-gather = s32[16,1,512]{2,1,0:T(1,128)S(1)} all-gather(s32[1,1,512]{2,1,0:T(1,128)S(1)} %bitcast.32), channel_id=1, replica_groups=mesh['blk'=16,'dp'=16] {'blk'}, dimensions={0}, use_global_device_ids=true | all-gather | bytes 34816 | tf_op jit(solution)/shard_map/all_gather | solution.py:40
  57.1 0.0 copy-done.1
  57.1 0.0 copy-start.8
  57.1 0.0 copy-start.5
  57.1 0.0 copy-start.6
  57.2 32.9 %gather_fusion = f32[8192]{0:T(1024)S(1)} fusion(f32[1024]{0:T(1024)S(1)} %copy-done.1, s32[8192]{0:T(1024)S(1)} %fusion.22), kind=kCustom, calls=%fused_computation | custom fusion | bytes 98304 | tf_op jit(solution)/shard_map/jit(_take)/gather | solution.py:42
  90.0 0.0 copy-done.8
  90.0 0.0 copy-start.13
  90.1 0.4 fusion.5
  90.5 0.0 copy-start.4
  90.5 1.0 copy-done.4
  91.5 0.0 copy-done.5
  91.5 0.0 copy-done.6
  91.5 1.1 fusion.13
  92.7 0.0 all-to-all-done
  92.7 0.0 all-gather.3.cloned.1.call-done
  92.7 0.0 copy-done.13
  92.7 6.7 %fusion.28 = (f32[256]{0:T(256)S(1)}, f32[256,8192]{0,1:T(8,128)S(1)}) fusion(f32[8192]{0:T(1024)S(1)} %and_select_fusion, bf16[8192,256]{1,0:T(8,128)(2,1)} %all-gather.3.cloned.1.call-done, bf16[256,256]{1,0:T(8,128)(2,1)S(1)} %copy-done.6, s32[256]{0:T(256)S(1)} %copy-done.13, s32[8192]{0:T(1024)S(1)} %bitcast.31), kind=kOutput, calls=%fused_computation.43 | convolution fusion | flops 1084227328 | bytes 12781568 | tf_op jit(solution)/shard_map/dot_general | solution.py:44
  99.4 0.8 divide_convert_fusion
  100.2 0.0 copy-start.2
  100.2 1.9 copy-done.2
  102.2 4.5 convolution_multiply_fusion
  106.6 0.0 reduce-scatter.2.cloned.1.call-update
  106.7 0.0 all-reduce.3.cloned.1.call-start
  106.7 1.8 fusion.18
  108.5 3.7 fusion.7
  112.2 0.0 copy-start.10
  112.2 93.7 %reduce-scatter.2.cloned.1.call-done = f32[512,256]{1,0:T(8,128)} async-done(((f32[8192,256]{1,0:T(8,128)}), f32[512,256]{1,0:T(8,128)}) %reduce-scatter.2.cloned.1.call-update) | async-done | bytes 524304 | tf_op jit(solution)/shard_map/reduce_scatter | solution.py:53
  205.9 3.8 convolution_add_fusion
  209.6 0.0 copy-done.10
  209.6 5.3 %fusion.4 = f32[256,2048]{0,1:T(8,128)} fusion(f32[2048,256]{1,0:T(8,128)} %fusion.7, bf16[512,256]{1,0:T(8,128)(2,1)S(1)} %copy-done.10, bf16[512,2048]{1,0:T(8,128)(2,1)} %copy-done.3, bf16[2048,256]{1,0:T(8,128)(2,1)} %param.17, f32[512,256]{1,0:T(8,128)} %reduce-scatter.2.cloned.1.call-done), kind=kOutput, calls=%fused_computation.13 | convolution fusion | flops 1077542912 | bytes 8126464 | tf_op jit(solution)/shard_map/dot_general | solution.py:22
  214.9 0.0 copy-start.9
  214.9 0.0 all-reduce.3.cloned.1.call-update
  215.0 0.9 copy-done.9
  215.9 5.4 %fusion.8 = f32[256,256]{1,0:T(8,128)} fusion(bf16[256,8192]{0,1:T(8,128)(2,1)} %copy-done.2, bf16[8192,256]{1,0:T(8,128)(2,1)} %all-gather.3.cloned.1.call-done, f32[256,256]{1,0:T(8,128)S(1)} %copy-done.9, f32[256]{0:T(256)S(1)} %get-tuple-element.14), kind=kOutput, calls=%fused_computation.20 | convolution fusion | flops 1073938432 | bytes 8913920 | tf_op jit(solution)/shard_map/dot_general | solution.py:50
  221.3 261.8 %all-reduce.3.cloned.1.call-done = (f32[256,2048]{0,1:T(8,128)}, f32[2048,256]{1,0:T(8,128)}) async-done(((f32[256,2048]{0,1:T(8,128)}, f32[2048,256]{1,0:T(8,128)}), (f32[256,2048]{0,1:T(8,128)}, f32[2048,256]{1,0:T(8,128)})) %all-reduce.3.cloned.1.call-update) | async-done | bytes 4194320 | tf_op jit(solution)/shard_map/psum | solution.py:64
  483.1 0.0 copy-start.7
  483.2 3.0 copy.14
  486.2 0.0 copy-done.7
  486.2 1.3 copy.22
  (3 shorter events, 0.0 us)
Async XLA Ops:
  7.2 1.2 copy-start
  7.2 6.9 %copy-start.11 = (s32[512]{0:T(512)S(1)}, s32[512]{0:T(512)}, u32[]{:S(2)}) copy-start(s32[512]{0:T(512)} %param.13) | copy-start | bytes 6148
  7.2 17.5 %copy-start.12 = (s32[512]{0:T(512)S(1)}, s32[512]{0:T(512)}, u32[]{:S(2)}) copy-start(s32[512]{0:T(512)} %param.14) | copy-start | bytes 6148
  7.2 49.9 %copy-start.1 = (f32[1024]{0:T(1024)S(1)}, f32[1024]{0:T(1024)}, u32[]{:S(2)}) copy-start(f32[1024]{0:T(1024)} %param.15) | copy-start | bytes 12292
  7.2 85.5 %all-gather.3.cloned.1.call-start = ((), (), s32[]{:S(2)}) async-start(), calls=%async_computation.2 | async-start | bytes 4456448 | tf_op jit(solution)/shard_map/all_gather | solution.py:36
  10.1 1.3 copy-start.3
  14.7 78.0 %all-to-all-start = ((s32[16,1,512]{2,1,0:T(1,128)}), s32[16,1,512]{2,1,0:T(1,128)S(1)}, u32[]{:S(2)}, u32[]{:S(2)}) async-start(s32[16,1,512]{2,1,0:T(1,128)} %stack.2), calls=%async_computation | async-start | bytes 65536 | tf_op jit(solution)/shard_map/all_to_all | solution.py:38
  24.6 181.2 %reduce-scatter.2.cloned.1.call-start = ((), (), s32[]{:S(2)}) async-start(), calls=%async_computation.3 | async-start | bytes 8912896 | tf_op jit(solution)/shard_map/reduce_scatter | solution.py:53
  57.1 32.9 %copy-start.8 = (bf16[256,256]{1,0:T(8,128)(2,1)S(1)}, bf16[256,256]{1,0:T(8,128)(2,1)}, u32[]{:S(2)}) copy-start(bf16[256,256]{1,0:T(8,128)(2,1)} %param.10) | copy-start | bytes 393220
  57.1 34.4 %copy-start.5 = (bf16[2048,256]{1,0:T(8,128)(2,1)S(1)}, bf16[2048,256]{1,0:T(8,128)(2,1)}, u32[]{:S(2)}) copy-start(bf16[2048,256]{1,0:T(8,128)(2,1)} %param.17) | copy-start | bytes 3145732
  57.1 34.4 %copy-start.6 = (bf16[256,256]{1,0:T(8,128)(2,1)S(1)}, bf16[256,256]{1,0:T(8,128)(2,1)}, u32[]{:S(2)}) copy-start(bf16[256,256]{1,0:T(8,128)(2,1)} %param.9) | copy-start | bytes 393220
  90.0 2.6 copy-start.13
  90.5 1.0 copy-start.4
  100.2 1.9 copy-start.2
  106.7 376.5 %all-reduce.3.cloned.1.call-start = ((), (), s32[]{:S(2)}) async-start(), calls=%async_computation.4 | async-start | bytes 8388608 | tf_op jit(solution)/shard_map/psum | solution.py:64
  112.2 97.4 %copy-start.10 = (bf16[512,256]{1,0:T(8,128)(2,1)S(1)}, bf16[512,256]{1,0:T(8,128)(2,1)}, u32[]{:S(2)}) copy-start(bf16[512,256]{1,0:T(8,128)(2,1)} %param.12) | copy-start | bytes 786436
  214.9 0.9 copy-start.9
  483.1 3.0 copy-start.7
Sparse Core Ops, SparseCore 0:
  14.2 78.3 all-gather.2
  106.8 99.0 reduce-scatter.1
  215.1 268.0 all-reduce.2
